TPU v7x, 32 devices: a whole 2x2x4 slice. The times are simulated.
32 devices in a mesh: rep: 4 (over z), exp: 8 (over y, x, core).
Axes of the slice: x: 2, y: 2, z: 4, core: 2. Of those that a mesh axis runs over, the one named last changes fastest.
Arguments:
- tokens: bfloat16 [16384, 1024], P(('rep', 'exp')), may hold values from -6 to 6
- routes: int32 [16384, 1], P(('rep', 'exp')), may hold values from 0 to 7; in each aligned block of 512 rows (0 to 511, 512 to 1023, ...) at most 64 rows name the same one
- lengths: int32 [8], replicated, may hold values from 1024 to 2048
- centroids: float32 [8, 1024], P('exp'), may hold values from -0.125 to 0.125
- norm_gains: float32 [8, 2, 1024], P('exp'), may hold values from 0.1 to 1.9
- norm_biases: float32 [8, 2, 1024], P('exp'), may hold values from -4 to 4
- w_in: bfloat16 [8, 2, 1024, 4096], P('exp', None, None, 'rep'), may hold values from -0.1875 to 0.1875
- in_biases: float32 [8, 2, 4096], P('exp'), may hold values from -4 to 4
- w_out: bfloat16 [8, 2, 4096, 1024], P('exp', None, 'rep'), may hold values from -0.09375 to 0.09375
- out_biases: float32 [8, 2, 1024], P('exp'), may hold values from -4 to 4
- cotangent: bfloat16 [16384, 1024], P(('rep', 'exp')), may hold values from -6 to 6
Outputs:
- mixed: bfloat16 [16384, 1024], P(('rep', 'exp'))
- tokens_grad: bfloat16 [16384, 1024], P(('rep', 'exp'))
- centroid_grad: float32 [8, 1024], P('exp')
- gain_grad: float32 [8, 2, 1024], P('exp')
- norm_bias_grad: float32 [8, 2, 1024], P('exp')
- w_in_grad: float32 [8, 2, 1024, 4096], P('exp', None, None, 'rep')
- in_bias_grad: float32 [8, 2, 4096], P('exp')
- w_out_grad: float32 [8, 2, 4096, 1024], P('exp', None, 'rep')
- out_bias_grad: float32 [8, 2, 1024], P('exp')
Inputs may be any that keep to these rules, and one draw needn't show every extreme that they name: `routes`: within the token slots of one device, each expert is named by exactly 64 slots.
All inputs are finite; a program needn't handle non-finite values.
Results may differ from a plain program's by a relative error of at most 0.0068.
Values may be sent and summed in bfloat16 or wider, within the bound.
A program may use at most 256 MiB of HBM per device.

v0:
```python
import functools

import jax
import jax.numpy as jnp
from jax import lax
from jax.experimental import pallas as pl
from jax.experimental.pallas import tpu as pltpu
from jax.sharding import PartitionSpec as P

eps = 1e-05
VMEM_BYTES = 44 * 1024 * 1024


def contract_rows(left, right):
    return lax.dot_general(
        left, right, (((0,), (0,)), ((), ())), preferred_element_type=jnp.float32
    )


def contract_cols(left, right):
    return lax.dot_general(
        left, right, (((1,), (1,)), ((), ())), preferred_element_type=jnp.float32
    )


MESH = pl.DeviceIdType.MESH
POOL = 4
PLANS = {448: (32, 32, 32, 16), 512: (64, 64)}
SPARE = 16
ORDER = (0, 2, 4, 6, 5, 7, 3, 1)
ROOT = 0.7978845608028654
CUBE = 0.044715


def layer_stats(values):
    center = values - jnp.mean(values, -1, keepdims=True)
    spread = jnp.mean(center * center, -1, keepdims=True)
    scale = lax.rsqrt(spread + eps)
    return center * scale, scale


def gelu_and_slope(inner):
    square = inner * inner
    bent = jnp.tanh(inner * (ROOT + (ROOT * CUBE) * square))
    half = 0.5 * (1.0 + bent)
    slope = half + (0.5 * inner) * (1.0 - bent * bent) * (ROOT + (3.0 * ROOT * CUBE) * square)
    return inner * half, slope


def fold(rows):
    return jnp.sum(rows.reshape(rows.shape[0] // 8, 8, rows.shape[1]), 0)


def pair_of(b):
    return (b >> 2) * 2 + (b & 1)


def flip(index, bits):
    out, place = index, 1
    while place <= bits:
        if bits & place:
            out = out + place * (1 - 2 * lax.rem(index // place, 2))
        place *= 2
    return out


def slot_rows(routes, blocks, cap):
    rows = routes.shape[1]
    along = routes.astype(jnp.float32)
    table = lax.broadcasted_iota(jnp.int32, (max(blocks, 8), rows), 0).astype(jnp.float32)
    hits = (table == along).astype(jnp.float32)
    first = lax.broadcasted_iota(jnp.int32, (rows, rows), 0)
    second = lax.broadcasted_iota(jnp.int32, (rows, rows), 1)
    earlier = (first < second).astype(jnp.bfloat16)
    before = jnp.dot(hits.astype(jnp.bfloat16), earlier, preferred_element_type=jnp.float32)
    target = along * cap + jnp.sum(before * hits, 0, keepdims=True)
    return (first.astype(jnp.float32) == target).astype(jnp.bfloat16)


def live_count(lengths_ref, device, devices, rows):
    slot = rows * devices // lengths_ref.shape[0]
    start = device * rows
    return lengths_ref[start // slot] - lax.rem(start, slot)


def live_rows(lengths_ref, device, devices, rows):
    count = live_count(lengths_ref, device, devices, rows)
    return (lax.broadcasted_iota(jnp.int32, (rows, 1), 0) < count).astype(jnp.float32)


def kernel(n, blocks, inside, parts, *refs):
    refs = list(refs)
    take = lambda count: [refs.pop(0) for _ in range(count)]
    if inside:
        tok_ref, cot_hbm, routes_ref, lengths_ref = take(4)
    else:
        x_ref, dy_ref = take(2)
    gain_ref, nbias_ref, cent_ref, bias_ref, bout_ref, wi_hbm, wo_hbm = take(7)
    home_y, home_dv, gwi, gwo, cent_out, gain_out, nbias_out, bin_out, bout_out = take(9)
    top_out = take(1)[0] if inside else None
    gath, wi, wo, part, act, dq, slope, total, state, dlog, recv, stage = take(12)
    accs, bacc, mine, peers, mine_late, peers_late = take(6)
    send_sem, recv_sem, load_sem, peer_send, peer_recv = take(5)
    if inside:
        x_ref, dy_ref, y_ref, dv_ref, place, cot_ref, part_x, part_dy, pack, seen, top = take(11)
        out_x, out_dy = y_ref, dv_ref
        out_send, out_recv, home_send, home_recv, home_own, cot_sem = take(6)
        seen_send, seen_recv = take(2)
    else:
        y_ref, dv_ref = home_y, home_dv
    r = lax.axis_index("rep")
    e = lax.axis_index("exp")
    own_rows, width = x_ref.shape
    hidden = wi_hbm.shape[2]
    rows = home_y.shape[0]
    cap = rows // blocks
    chunk = sum(parts)
    CHUNKS = own_rows // chunk
    starts = [sum(parts[:h]) for h in range(len(parts))]
    every = range(len(parts))
    ops = 4 * CHUNKS
    rounds = ops + 1
    wtile = hidden // 4
    last = n - 1

    def op_type(i):
        return jnp.where(i < CHUNKS, 0, jnp.where(i >= 3 * CHUNKS, 3, 1 + lax.rem(i + CHUNKS, 2)))

    def op_chunk(i):
        return jnp.where(
            i < CHUNKS, i, jnp.where(i >= 3 * CHUNKS, i - 3 * CHUNKS, (i - CHUNKS) // 2)
        )

    def op_slot(i):
        return jnp.where(i < CHUNKS, i, CHUNKS + lax.rem(i, POOL))

    def half_rows(h):
        return pl.ds(starts[h], parts[h])

    def extent(h):
        return (0, chunk) if h is None else (starts[h], parts[h])

    def block_of(h):
        return 32 if extent(h)[1] % 32 == 0 else 16

    ahead = (jnp.minimum(r + 1, last), jnp.maximum(r - 1, 0))
    pos = (r, last - r)

    def item_sent(d, s):
        return lax.rem(r - s + n, n) if d == 0 else lax.rem(r + s, n)

    def sends(d, k, s):
        return (pos[d] < last) & jnp.where(s <= pos[d], k < ops, k >= 1)

    def receives(d, k, s):
        return (pos[d] > 0) & jnp.where(s <= pos[d] - 1, k < ops, k >= 1)

    def copy(d, k, s, h, src, dst):
        return pltpu.make_async_remote_copy(
            src_ref=src,
            dst_ref=dst,
            send_sem=send_sem.at[d, lax.rem(s, 2), h],
            recv_sem=recv_sem.at[d, lax.rem(k, 2), s, h],
            device_id={"rep": ahead[d]},
            device_id_type=MESH,
        )

    def landing(d, k, s, h):
        return recv.at[d, lax.rem(k, 2), s, half_rows(h)]

    def staged(d, s, h):
        return stage.at[d, lax.rem(s, 2), half_rows(h)]

    def wait_sent(d, k, s, h):
        @pl.when(sends(d, k, s))
        def _():
            copy(d, k, s, h, staged(d, s, h), landing(d, k, s, h)).wait_send()

    def wait_received(d, k, s, h):
        @pl.when(receives(d, k, s))
        def _():
            copy(d, k, s, h, staged(d, s, h), landing(d, k, s, h)).wait_recv()

    def finish_sum(k, h):
        rs = half_rows(h)
        total[rs, :] = part[r, rs, :]
        for d in range(2):

            @pl.when(pos[d] > 0)
            def _():
                total[rs, :] += landing(d, k, n - 1, h)[...].astype(jnp.float32)

    def send(d, k, s, h):
        gathers = s <= pos[d]
        p = item_sent(d, s)
        rs = half_rows(h)

        @pl.when(sends(d, k, s) & gathers)
        def _():
            here = gath.at[op_slot(k), p, rs]
            copy(d, k, s, h, here, here).start()

        @pl.when(sends(d, k, s) & jnp.logical_not(gathers))
        def _():
            out = staged(d, s, h)

            @pl.when(pos[d] == 0)
            def _():
                out[...] = part[p, rs, :].astype(jnp.bfloat16)

            @pl.when(pos[d] > 0)
            def _():
                came = landing(d, k, s - 1, h)[...].astype(jnp.float32)
                out[...] = (part[p, rs, :] + came).astype(jnp.bfloat16)

            copy(d, k, s, h, out, landing(d, k, s, h)).start()

    def over_blocks(h, body):
        size = block_of(h)

        def step(b, carry):
            body(pl.multiple_of(extent(h)[0] + b * size, 16))
            return carry

        lax.fori_loop(0, extent(h)[1] // size, step, 0)

    side = lax.rem(e // 2, 2)
    full_at = (0, own_rows - cap, cap, own_rows - 2 * cap)
    middle = pl.ds(2 * cap, own_rows - 4 * cap)

    def cap_rows(q):
        return pl.ds(pl.multiple_of(q * cap, cap), cap)

    def out_copy(w, b, kind):
        j = pair_of(b)
        src = (out_x, out_dy)[w]
        dst = ((x_ref, part_x), (dy_ref, part_dy))[w][kind]
        return pltpu.make_async_remote_copy(
            src_ref=src.at[cap_rows(b)],
            dst_ref=dst.at[pl.ds((full_at[j], j * cap)[kind], cap)],
            send_sem=out_send.at[w, b],
            recv_sem=out_recv.at[w, kind, j],
            device_id={"exp": flip(e, b)},
            device_id_type=MESH,
        )

    def results_of(w, j, kind):
        src = ((y_ref, part_x), (dv_ref, part_dy))[w][kind]
        return src.at[pl.ds((full_at[j], j * cap)[kind], cap)]

    def home_copy(w, j, kind):
        return pltpu.make_async_remote_copy(
            src_ref=results_of(w, j, kind),
            dst_ref=(home_y, home_dv)[w].at[cap_rows(e)],
            send_sem=home_send.at[w, kind, j],
            recv_sem=home_recv.at[w, side, j],
            device_id={"exp": flip(e, 4 * (j // 2) + j % 2) + 2 * (kind - side)},
            device_id_type=MESH,
        )

    def home_own_copy(w, kind):
        dst = (home_y, home_dv)[w].at[cap_rows(e)]
        return pltpu.make_async_copy(results_of(w, 0, kind), dst, home_own.at[w])

    def await_home(w, j, expert_side):
        pltpu.make_async_remote_copy(
            src_ref=part_x.at[pl.ds(0, cap)],
            dst_ref=(home_y, home_dv)[w].at[cap_rows(0)],
            send_sem=home_send.at[w, 0, j],
            recv_sem=home_recv.at[w, expert_side, j],
            device_id={"exp": flip(e, 1)},
            device_id_type=MESH,
        ).wait_recv()

    def per_kind(body):
        for kind in range(2):

            @pl.when(side == kind)
            def _():
                body(kind)

    def dispatch(w, first, stop):
        values = (tok_ref, cot_ref)[w][...]
        if w == 1:
            device = r * blocks + e
            live = live_rows(lengths_ref, device, n * blocks, rows)
            values = (live * values.astype(jnp.float32)).astype(jnp.bfloat16)
        for b in ORDER[first:stop]:
            picked = place[cap_rows(flip(e, b)), :]
            ordered = jnp.dot(picked, values, preferred_element_type=jnp.float32)
            ordered = ordered.astype(jnp.bfloat16)
            if b == 0:

                @pl.when(side == 0)
                def _():
                    (x_ref, dy_ref)[w][:cap, :] = ordered

                @pl.when(side == 1)
                def _():
                    (part_x, part_dy)[w][:cap, :] = ordered

            else:
                (out_x, out_dy)[w][cap_rows(b), :] = ordered
                if w == 0 and b == ORDER[1]:
                    pl.semaphore_wait(barrier, n - 1 + blocks - 1)
                per_kind(lambda kind: out_copy(w, b, kind).start())

    def await_block(w, kind, j):
        def wait():
            out_copy(w, 4 * (j // 2) + j % 2 + 2, kind).wait_recv()

        if j:
            wait()
        else:
            pl.when(side != kind)(wait)

    def seen_copy(b):
        return pltpu.make_async_remote_copy(
            src_ref=seen.at[0],
            dst_ref=seen.at[b],
            send_sem=seen_send.at[b],
            recv_sem=seen_recv.at[b],
            device_id={"exp": flip(e, b)},
            device_id_type=MESH,
        )

    def count_live():
        count = live_count(lengths_ref, r * blocks + e, n * blocks, rows)
        live = lax.broadcasted_iota(jnp.int32, (blocks, rows), 1) < count
        table = lax.broadcasted_iota(jnp.int32, (blocks, rows), 0)
        hits = jnp.where((table == routes_ref[...]) & live, 1.0, 0.0)
        seen[0] = jnp.broadcast_to(jnp.sum(hits, 1, keepdims=True), (blocks, 128))
        for b in range(1, blocks):
            seen_copy(b).start()

    def fullest():
        for b in range(1, blocks):
            seen_copy(b).wait_recv()
        total_seen = seen[0]
        for b in range(1, blocks):
            total_seen += seen[b]
        top[...] = jnp.max(total_seen, 0, keepdims=True)

    def make_pack():
        lane = lax.broadcasted_iota(jnp.int32, (1, 4 * cap), 1)
        target = jnp.zeros((1, 4 * cap), jnp.float32)
        before = jnp.zeros((1, 1), jnp.float32)
        for j in range(4):
            from_it = 4 * (j // 2) + j % 2 + 2 * (1 - side)
            count = seen[from_it, pl.ds(e, 1), 0:1]
            within = (lane - j * cap).astype(jnp.float32)
            here = (lane >= j * cap) & (lane < (j + 1) * cap)
            at = jnp.where(within < count, within + before, -1.0)
            target = jnp.where(here, at, target)
            before += count
        row = lax.broadcasted_iota(jnp.int32, (own_rows - 4 * cap, 4 * cap), 0)
        pack[...] = (row.astype(jnp.float32) == target).astype(jnp.bfloat16)

    def pack_middle(w):
        landed, packed = ((part_x, x_ref), (part_dy, dy_ref))[w]
        packed[middle, :] = jnp.dot(
            pack[...], landed[...], preferred_element_type=jnp.float32
        ).astype(jnp.bfloat16)

    def unpack_middle(w):
        landed, packed = ((part_x, y_ref), (part_dy, dv_ref))[w]
        landed[...] = contract_rows(pack[...], packed[middle, :]).astype(jnp.bfloat16)

    def at_half(stop):
        c, offset = divmod(stop - 1, chunk)
        return c, max(h for h in every if starts[h] <= offset)

    def send_home(w, j, kind):
        if j:
            home_copy(w, j, kind).start()
        else:
            pl.when(side == kind)(lambda: home_own_copy(w, kind).start())
            pl.when(side != kind)(lambda: home_copy(w, 0, kind).start())

    def go_home(w, c, h):
        if not inside:
            return
        for chunk_at in range(CHUNKS):
            done = [j for j in range(4) if at_half(full_at[j] + cap) == (chunk_at, h)]
            packed = at_half(own_rows - 2 * cap) == (chunk_at, h)
            if done or packed:

                @pl.when(c == chunk_at)
                def _():
                    for j in done:
                        send_home(w, j, 0)
                    if packed:
                        unpack_middle(w)
                        for j in range(4):
                            send_home(w, j, 1)

    def gate_of(x):
        return jax.nn.sigmoid(jnp.sum(x * cent_ref[...], -1, keepdims=True))

    def prepare(i, h):
        kind, c, slot = op_type(i), op_chunk(i), op_slot(i)

        block = block_of(h)

        def own(offset, value):
            gath[slot, r, pl.ds(offset, block), :] = value.astype(jnp.bfloat16)

        def source(offset):
            return pl.ds(pl.multiple_of(c * chunk + offset, 16), block)

        @pl.when(kind == 0)
        def _():
            over_blocks(
                h,
                lambda o: own(
                    o,
                    layer_stats(x_ref[source(o), :].astype(jnp.float32))[0] * gain_ref[0:1, :]
                    + nbias_ref[0:1, :],
                )
            )

        @pl.when(kind == 1)
        def _():
            over_blocks(
                h,
                lambda o: own(
                    o, layer_stats(state[source(o), :])[0] * gain_ref[1:2, :] + nbias_ref[1:2, :]
                )
            )

        @pl.when(kind == 2)
        def _():
            over_blocks(
                h,
                lambda o: own(
                    o,
                    gate_of(x_ref[source(o), :].astype(jnp.float32))
                    * dy_ref[source(o), :].astype(jnp.float32),
                )
            )

        @pl.when(kind == 3)
        def _():
            over_blocks(h, lambda o: own(o, state[source(o), :]))

    def norm_back(values, grad, k):
        unit, scale = layer_stats(values)
        accs[1 + k] += fold(grad * unit)
        accs[3 + k] += fold(grad)
        through = grad * gain_ref[k : k + 1, :]
        return scale * (
            through
            - jnp.mean(through, -1, keepdims=True)
            - unit * jnp.mean(through * unit, -1, keepdims=True)
        )

    def finish(i, h):
        kind, c = op_type(i), op_chunk(i)
        block = block_of(h)

        def source(offset):
            return pl.ds(pl.multiple_of(c * chunk + offset, 16), block)

        @pl.when(kind == 0)
        def _():
            def body(o):
                state[source(o), :] = (
                    x_ref[source(o), :].astype(jnp.float32)
                    + total[pl.ds(o, block), :]
                    + bout_ref[0:1, :]
                )

            over_blocks(h, body)

        @pl.when(kind == 1)
        def _():
            def body(o):
                x = x_ref[source(o), :].astype(jnp.float32)
                dy = dy_ref[source(o), :].astype(jnp.float32)
                upper = state[source(o), :] + total[pl.ds(o, block), :] + bout_ref[1:2, :]
                gate = gate_of(x)
                y_ref[source(o), :] = (gate * upper).astype(jnp.bfloat16)
                logit = jnp.sum(dy * upper, -1, keepdims=True) * gate * (1.0 - gate)
                dlog[source(o), :] = jnp.broadcast_to(logit, (block, dlog.shape[1]))
                accs[0] += fold(logit * x)

            over_blocks(h, body)
            for part_at in every if h is None else [h]:
                go_home(0, c, part_at)

        @pl.when(kind == 2)
        def _():
            def body(o):
                x = x_ref[source(o), :].astype(jnp.float32)
                top = gate_of(x) * dy_ref[source(o), :].astype(jnp.float32)
                middle = top + norm_back(state[source(o), :], total[pl.ds(o, block), :], 1)
                state[source(o), :] = middle
                accs[5] += fold(middle)
                accs[6] += fold(top)

            over_blocks(h, body)

        @pl.when(kind == 3)
        def _():
            def body(o):
                x = x_ref[source(o), :].astype(jnp.float32)
                dv_ref[source(o), :] = (
                    state[source(o), :]
                    + norm_back(x, total[pl.ds(o, block), :], 0)
                    + dlog[source(o), 0:1] * cent_ref[...]
                ).astype(jnp.bfloat16)

            over_blocks(h, body)
            for part_at in every if h is None else [h]:
                go_home(1, c, part_at)

    def item_first(i, par, p):
        kind = op_type(i)
        k = jnp.where((kind == 1) | (kind == 2), 1, 0)
        slot = jnp.where(
            kind == 2, op_slot(i - 1), jnp.where(kind == 3, op_chunk(i), op_slot(i))
        )

        inner = (
            jnp.dot(gath[slot, p], wi[k], preferred_element_type=jnp.float32)
            + bias_ref[pl.ds(k, 1), pl.ds(pl.multiple_of(r * hidden, hidden), hidden)]
        )
        low, pull = gelu_and_slope(inner)
        act[par, p] = low.astype(jnp.bfloat16)
        slope[...] = pull

    def item_pull(i, par, p):
        kind = op_type(i)
        k = jnp.where((kind == 1) | (kind == 2), 1, 0)

        @pl.when(kind >= 2)
        def _():
            grad = contract_cols(gath[op_slot(i), p], wo[k]) * slope[...]
            bacc[k] += fold(grad)
            dq[par, p] = grad.astype(jnp.bfloat16)

    def item_second(i, par, p):
        kind = op_type(i)
        k = jnp.where((kind == 1) | (kind == 2), 1, 0)

        @pl.when(kind < 2)
        def _():
            part[p] = jnp.dot(act[par, p], wo[k], preferred_element_type=jnp.float32)

        @pl.when(kind >= 2)
        def _():
            part[p] = contract_cols(dq[par, p], wi[k])

    def weight_grads(i, par, j):
        kind = op_type(i)
        k = jnp.where(kind == 2, 1, 0)
        slot = jnp.where(kind == 2, op_slot(i - 1), op_chunk(i))
        cs = pl.ds(pl.multiple_of(j * wtile, wtile), wtile)
        depth = n * chunk
        normed = gath[slot, :, :, cs].reshape(depth, wtile)
        gwi[k, cs, :] += contract_rows(normed, dq[par].reshape(depth, hidden))
        active = act[par, :, :, cs].reshape(depth, wtile)
        gwo[k, cs, :] += contract_rows(active, gath[op_slot(i)].reshape(depth, width))

    def item_at(s):
        near = jnp.minimum(r, last - r)
        base = jnp.where(near == 0, last - s, jnp.where(s < 2, last - s, s - 2))
        return jnp.where(r < 2, base, last - base)

    def cot_load():
        return pltpu.make_async_copy(cot_hbm, cot_ref, cot_sem)

    EARLY, LATE = (0, 2, 4, 5, 6), (1, 3)

    def tell(late, q):
        src, dst = ((mine, peers), (mine_late, peers_late))[late]
        return pltpu.make_async_remote_copy(
            src_ref=src,
            dst_ref=dst.at[q - 1],
            send_sem=peer_send.at[late, q - 1],
            recv_sem=peer_recv.at[late, q - 1],
            device_id={"rep": lax.rem(r + q, n)},
            device_id_type=MESH,
        )

    def tell_early():
        for a, row in enumerate(EARLY):
            mine[a : a + 1, :width] = jnp.sum(accs[row], 0, keepdims=True)
        mine[5:6, :hidden] = jnp.sum(bacc[1], 0, keepdims=True)
        mine[6:8, :] = jnp.zeros((2, mine.shape[1]), jnp.float32)
        if inside:
            mine[6:7, :128] = top[...]
        for q in range(1, n):
            tell(0, q).start()

    def tell_late():
        at = 0
        for values in (accs[LATE[0]], accs[LATE[1]], bacc[0]):
            flat = jnp.sum(values, 0, keepdims=True)
            for j in range(flat.shape[1] // 128):
                mine_late[at : at + 1, :] = flat[:, j * 128 : (j + 1) * 128]
                at += 1
        for q in range(1, n):
            tell(1, q).start()

    def unpack(packed, at, size):
        return jnp.concatenate([packed[at + j : at + j + 1] for j in range(size // 128)], 1)

    def load(w):
        src, dst = ((wi_hbm, wi), (wo_hbm, wo))[w]
        return pltpu.make_async_copy(src, dst, load_sem.at[w])

    barrier = pltpu.get_barrier_semaphore()
    for q in range(1, n):
        pl.semaphore_signal(
            barrier, inc=1, device_id={"rep": lax.rem(r + q, n)}, device_id_type=MESH
        )
    load(0).start()
    load(1).start()
    if inside:
        for b in range(1, blocks):
            pl.semaphore_signal(
                barrier, inc=1, device_id={"exp": flip(e, b)}, device_id_type=MESH
            )
        cot_load().start()
        place[...] = slot_rows(routes_ref[...], blocks, cap)
        dispatch(0, 0, 2)
        await_block(0, 0, 0)
    else:
        pl.semaphore_wait(barrier, n - 1)
    prepare(0, 0)

    def step(t, carry):
        k, s = t // n, lax.rem(t, n)
        k_before, s_before = (t - 1) // n, lax.rem(t + n - 1, n)
        i = k - 1
        par = lax.rem(k, 2)
        p = item_at(s)

        def exchange(h):
            for d in range(2):

                @pl.when(t >= 1)
                def _():
                    wait_received(d, k_before, s_before, h)

                @pl.when(t >= 2)
                def _():
                    wait_sent(d, (t - 2) // n, lax.rem(t + n - 2, n), h)

            @pl.when((s == 0) & (k >= 2))
            def _():
                finish_sum(k - 1, h)

            for d in range(2):
                send(d, k, s, h)

        def grads(j):
            old = k - 2

            @pl.when((s < 2) & (old >= CHUNKS) & (op_type(old) >= 2))
            def _():
                weight_grads(old, lax.rem(k + 1, 2), j)

        exchange(0)

        @pl.when(t == n * ops)
        def _():
            tell_early()

        @pl.when(t == 0)
        def _():
            if inside:
                dispatch(0, 2, blocks)
                await_block(0, 0, 2)
            for h in every[1:]:
                prepare(0, h)

        @pl.when(t == 1)
        def _():
            def clear(b, carry):
                zero_rows = pl.ds(pl.multiple_of(b * 64, 64), 64)
                for w in range(2):
                    gwi[w, zero_rows, :] = jnp.zeros((64, hidden), jnp.float32)
                    gwo[w, zero_rows, :] = jnp.zeros((64, width), jnp.float32)
                return carry

            lax.fori_loop(0, width // 64, clear, 0)
            accs[...] = jnp.zeros_like(accs)
            bacc[...] = jnp.zeros_like(bacc)

        if inside:

            @pl.when(t == 2)
            def _():
                cot_load().wait()
                dispatch(1, 0, blocks)

            @pl.when(t == 1)
            def _():
                count_live()

            @pl.when(t == 3)
            def _():
                fullest()
                make_pack()
                for kind, j in ((0, 1), (0, 3), (1, 0), (1, 1), (1, 2), (1, 3)):
                    await_block(0, kind, j)
                pack_middle(0)

            @pl.when(t == n * CHUNKS)
            def _():
                for w in range(2):
                    for b in range(1, blocks):
                        out_copy(w, b, 0).wait_send()
                for b in range(1, blocks):
                    seen_copy(b).wait_send()
                for kind in range(2):
                    for j in range(4):
                        await_block(1, kind, j)
                pack_middle(1)

        @pl.when(t == n)
        def _():
            load(0).wait()
            load(1).wait()

        pieces = [item_first, item_pull, item_second]
        for h in every:
            if h:
                exchange(h)
            mine_now = pieces[h : h + 1] if h < len(parts) - 1 else pieces[h:]
            if len(parts) == 2:
                mine_now = (pieces[:2], pieces[2:])[h]

            @pl.when(k >= 1)
            def _():
                for piece in mine_now:
                    piece(i, par, p)

            if h == 0:
                grads(2 * s)
            elif h == len(parts) - 1:
                grads(2 * s + 1)

        @pl.when((s == 2) & (k >= 2))
        def _():
            finish(k - 2, None)

        @pl.when((s == 3) & (k < ops - 1))
        def _():
            prepare(k + 1, None)

        return carry

    steps = rounds * n
    lax.fori_loop(0, steps, step, 0)

    def last_grads(j, carry):
        weight_grads(ops - 1, (rounds - 1) % 2, j)
        return carry

    lax.fori_loop(0, 4, last_grads, 0)
    for h in every:
        for d in range(2):
            wait_received(d, rounds - 1, n - 1, h)
        finish_sum(rounds - 1, h)
        finish(ops - 1, h)
    for h in every:
        for d in range(2):
            for back in (2, 1):
                wait_sent(d, (steps - back) // n, (steps - back) % n, h)

    tell_late()

    def place_bins(k, q, bins):
        bin_out[k : k + 1, pl.ds(pl.multiple_of(q * hidden, hidden), hidden)] = bins

    for q in range(1, n):
        tell(0, q).wait_recv()
    sums = mine[0:5, :width]
    place_bins(1, r, mine[5:6, :hidden])
    for q in range(1, n):
        sums += peers[q - 1, 0:5, :width]
        place_bins(1, lax.rem(r - q + n, n), peers[q - 1, 5:6, :hidden])
    cent_out[...] = sums[0:1]
    gain_out[1:2, :] = sums[1:2]
    nbias_out[1:2, :] = sums[2:3]
    bout_out[...] = sums[3:5]
    if inside:
        most = mine[6:7, :128]
        for q in range(1, n):
            most = jnp.maximum(most, peers[q - 1, 6:7, :128])
        top_out[...] = jnp.broadcast_to(most, top_out.shape)
    for q in range(1, n):
        tell(1, q).wait_recv()
    mine_rows = mine_late[...]
    late = mine_rows[: 2 * width // 128]
    place_bins(0, r, unpack(mine_rows, 2 * width // 128, hidden))
    for q in range(1, n):
        theirs = peers_late[q - 1]
        late += theirs[: 2 * width // 128]
        place_bins(0, lax.rem(r - q + n, n), unpack(theirs, 2 * width // 128, hidden))
    gain_out[0:1, :] = unpack(late, 0, width)
    nbias_out[0:1, :] = unpack(late, width // 128, width)
    for q in range(1, n):
        tell(0, q).wait_send()
        tell(1, q).wait_send()
    if inside:
        for w in range(2):
            for kind in range(2):
                for j in range(4):
                    if j:
                        home_copy(w, j, kind).wait_send()
                    else:
                        pl.when(side == kind)(lambda: home_own_copy(w, kind).wait())
                        pl.when(side != kind)(lambda: home_copy(w, 0, kind).wait_send())
            for j in range(4):
                for expert_side in range(2):
                    if j:
                        await_home(w, j, expert_side)
                    else:
                        pl.when(side != expert_side)(
                            functools.partial(await_home, w, j, expert_side)
                        )


def run_layer(own_rows, name, inside, rows_in, gains, nbias, cent, biases, bout, wi, wo):
    n, blocks = lax.axis_size("rep"), lax.axis_size("exp")
    rows, width = rows_in[0].shape
    hidden = wi.shape[2]
    parts = PLANS[own_rows] if inside else (rows // 8, rows // 8)
    chunk = sum(parts)
    CHUNKS = own_rows // chunk
    wide = max(width, hidden)
    late = (2 * width + hidden) // 128
    low, full = jnp.bfloat16, jnp.float32
    vmem = pl.BlockSpec(memory_space=pltpu.VMEM)
    anywhere = pl.BlockSpec(memory_space=pl.ANY)
    row_specs = [vmem] * 2
    extra = []
    if inside:
        row_specs = [vmem, anywhere, vmem, pl.BlockSpec(memory_space=pltpu.SMEM)]
        extra = (
            [pltpu.VMEM((own_rows, width), low)] * 2
            + [pltpu.VMEM((rows, width), low)] * 2
            + [pltpu.VMEM((rows, rows), low)]
            + [pltpu.VMEM((rows, width), low)]
            + [pltpu.VMEM((rows // 2, width), low)] * 2
            + [pltpu.VMEM((own_rows - rows // 2, rows // 2), low)]
            + [pltpu.VMEM((blocks, blocks, 128), full), pltpu.VMEM((1, 128), full)]
            + [pltpu.SemaphoreType.DMA((2, blocks)), pltpu.SemaphoreType.DMA((2, 2, blocks // 2))]
            + [pltpu.SemaphoreType.DMA((2, 2, blocks // 2))] * 2
            + [pltpu.SemaphoreType.DMA((2,)), pltpu.SemaphoreType.DMA]
            + [pltpu.SemaphoreType.DMA((blocks,))] * 2
        )
    flops = 2 * 16 * n * own_rows * width * hidden
    return pl.pallas_call(
        functools.partial(kernel, n, blocks, inside, parts),
        out_shape=(
            pltpu.VMEM((rows, width), low) if inside else jax.ShapeDtypeStruct((rows, width), low),
            pltpu.VMEM((rows, width), low) if inside else jax.ShapeDtypeStruct((rows, width), low),
            pltpu.VMEM((2, width, hidden), full),
            pltpu.VMEM((2, hidden, width), full),
            jax.ShapeDtypeStruct((1, width), full),
            jax.ShapeDtypeStruct((2, width), full),
            jax.ShapeDtypeStruct((2, width), full),
            jax.ShapeDtypeStruct((2, n * hidden), full),
            jax.ShapeDtypeStruct((2, width), full),
        )
        + ((jax.ShapeDtypeStruct((8, 128), full),) if inside else ()),
        in_specs=row_specs + [vmem] * 5 + [anywhere] * 2,
        out_specs=(vmem,) * (10 if inside else 9),
        scratch_shapes=[
            pltpu.VMEM((CHUNKS + POOL, n, chunk, width), low),
            pltpu.VMEM((2, width, hidden), low),
            pltpu.VMEM((2, hidden, width), low),
            pltpu.VMEM((n, chunk, width), full),
            pltpu.VMEM((2, n, chunk, hidden), low),
            pltpu.VMEM((2, n, chunk, hidden), low),
            pltpu.VMEM((chunk, hidden), full),
            pltpu.VMEM((chunk, width), full),
            pltpu.VMEM((own_rows, width), full),
            pltpu.VMEM((own_rows, 128), full),
            pltpu.VMEM((2, 2, n, chunk, width), low),
            pltpu.VMEM((2, 2, chunk, width), low),
            pltpu.VMEM((7, 8, width), full),
            pltpu.VMEM((2, 8, hidden), full),
            pltpu.VMEM((8, wide), full),
            pltpu.VMEM((n - 1, 8, wide), full),
            pltpu.VMEM((late, 128), full),
            pltpu.VMEM((n - 1, late, 128), full),
            pltpu.SemaphoreType.DMA((2, 2, len(parts))),
            pltpu.SemaphoreType.DMA((2, 2, n, len(parts))),
            pltpu.SemaphoreType.DMA((2,)),
            pltpu.SemaphoreType.DMA((2, n - 1)),
            pltpu.SemaphoreType.DMA((2, n - 1)),
        ]
        + extra,
        compiler_params=pltpu.CompilerParams(
            collective_id=name, has_side_effects=True, vmem_limit_bytes=VMEM_BYTES
        ),
        cost_estimate=pl.CostEstimate(
            flops=flops, bytes_accessed=40 * rows * width, transcendentals=8 * rows * hidden * n
        ),
    )(*rows_in, gains, nbias, cent, biases, bout, wi, wo)


def close_kernel(device_count, cap, *refs):
    tok_hbm, cot_hbm, routes_ref, lengths_ref, y, dv, gwi_in, gwo_in = refs[:8]
    small_in, refs = refs[8:13], refs[13:]
    mixed_ref, grad_ref, gwi_out, gwo_out = refs[:4]
    small_out, refs = refs[4:9], refs[9:]
    tok, cot, load_sem, move_sem = refs
    rows = tok.shape[0]
    loads = [
        pltpu.make_async_copy(src, dst, load_sem.at[j])
        for j, (src, dst) in enumerate(((tok_hbm, tok), (cot_hbm, cot)))
    ]
    moves = [
        pltpu.make_async_copy(src.at[k], dst.at[k], move_sem.at[w, k])
        for w, (src, dst) in enumerate(((gwi_in, gwi_out), (gwo_in, gwo_out)))
        for k in range(2)
    ]
    for copy in loads + moves:
        copy.start()
    for src, dst in zip(small_in, small_out):
        dst[...] = src[...]
    place = slot_rows(routes_ref[...], rows // cap, cap)
    device = lax.axis_index("rep") * lax.axis_size("exp") + lax.axis_index("exp")
    live = live_rows(lengths_ref, device, device_count, rows)
    for copy in loads:
        copy.wait()
    mixed_ref[...] = (tok[...].astype(jnp.float32) + live * contract_rows(place, y[...])).astype(
        jnp.bfloat16
    )
    grad_ref[...] = (cot[...].astype(jnp.float32) + contract_rows(place, dv[...])).astype(
        jnp.bfloat16
    )
    for copy in moves:
        copy.wait()


def close(tokens, cotangent, routes, lengths, home_y, home_dv, gwi, gwo, *small):
    n, blocks = lax.axis_size("rep"), lax.axis_size("exp")
    rows, width = tokens.shape
    vmem = pl.BlockSpec(memory_space=pltpu.VMEM)
    anywhere = pl.BlockSpec(memory_space=pl.ANY)
    rows_shape = jax.ShapeDtypeStruct(tokens.shape, tokens.dtype)
    like = lambda a: jax.ShapeDtypeStruct(a.shape, a.dtype)
    home_y, home_dv, gwi, gwo = (
        pltpu.with_memory_space_constraint(a, pltpu.VMEM) for a in (home_y, home_dv, gwi, gwo)
    )
    return pl.pallas_call(
        functools.partial(close_kernel, n * blocks, rows // blocks),
        out_shape=(rows_shape, rows_shape, like(gwi), like(gwo), *map(like, small)),
        in_specs=[anywhere, anywhere, vmem, pl.BlockSpec(memory_space=pltpu.SMEM)]
        + [vmem] * 9,
        out_specs=[vmem, vmem, anywhere, anywhere] + [vmem] * 5,
        scratch_shapes=[pltpu.VMEM((rows, width), tokens.dtype)] * 2
        + [pltpu.SemaphoreType.DMA((2,)), pltpu.SemaphoreType.DMA((2, 2))],
        compiler_params=pltpu.CompilerParams(vmem_limit_bytes=VMEM_BYTES),
    )(tokens, cotangent, routes, lengths, home_y, home_dv, gwi, gwo, *small)


def no_results(shapes):
    def kernel(*refs):
        refs[-1][...] = jnp.zeros_like(refs[-1])

    anywhere = pl.BlockSpec(memory_space=pl.ANY)
    *results, _ = pl.pallas_call(
        kernel,
        out_shape=(*shapes, jax.ShapeDtypeStruct((8, 128), jnp.float32)),
        out_specs=[anywhere] * len(shapes) + [pl.BlockSpec(memory_space=pltpu.VMEM)],
    )()
    return tuple(results)


def shards(
    tokens,
    routes,
    lengths,
    centroids,
    norm_gains,
    norm_biases,
    w_in,
    in_biases,
    w_out,
    out_biases,
    cotangent,
):
    n_exp = lax.axis_size("exp")
    tok_rows = tokens.shape[0]
    cap = tok_rows // n_exp
    params = (
        norm_gains[0],
        norm_biases[0],
        centroids,
        in_biases[0],
        out_biases[0],
        w_in[0],
        w_out[0],
    )
    devices = n_exp * lax.axis_size("rep")
    if n_exp == 8 and tok_rows == max(PLANS) and devices == 4 * lengths.shape[0]:
        less, whole = sorted(PLANS)
        given = (tokens, cotangent, routes.reshape(1, tok_rows), lengths)

        def layer(own_rows, name, given, *params):
            *results, most = run_layer(own_rows, name, True, given, *params)
            return tuple(close(*given, *results)), most[0, 0] <= own_rows

        seqs, planes = lengths.shape[0], lax.axis_size("rep")
        of_plane = lax.iota(jnp.int32, seqs) // (seqs // planes) == lax.iota(jnp.int32, planes)[:, None]
        plane_live = jnp.sum(jnp.where(of_plane, lengths, 0), 1)
        shapes = jax.eval_shape(functools.partial(layer, less, 0), given, *params)[0]
        results, done = lax.cond(
            jnp.max(plane_live) <= (less - SPARE) * n_exp,
            functools.partial(layer, less, 0),
            lambda *_: (no_results(shapes), jnp.array(False)),
            given,
            *params,
        )
        results = lax.cond(
            done,
            lambda results, *_: results,
            lambda results, *rest: layer(whole, 1, *rest)[0],
            results,
            given,
            *params,
        )
    else:
        device = lax.axis_index(("rep", "exp"))
        slot = tok_rows * n_exp * lax.axis_size("rep") // lengths.shape[0]
        positions = device * tok_rows + lax.iota(jnp.int32, tok_rows)
        seq_ids = positions // slot
        seq_table = lax.iota(jnp.int32, lengths.shape[0])
        seq_len = jnp.sum(
            jnp.where(seq_ids[:, None] == seq_table[None, :], lengths[None, :], 0), 1
        )
        live = (positions % slot < seq_len).astype(jnp.float32)[:, None]
        route = routes[:, 0]
        hits = (route[:, None] == lax.iota(jnp.int32, n_exp)[None, :]).astype(jnp.int32)
        before = jnp.cumsum(hits, 0) - hits
        target = route * cap + jnp.sum(before * hits, 1)
        place = (lax.iota(jnp.int32, tok_rows)[:, None] == target[None, :]).astype(jnp.bfloat16)
        grad_out = (live * cotangent.astype(jnp.float32)).astype(jnp.bfloat16)

        def send(rows):
            ordered = jnp.dot(place, rows, preferred_element_type=jnp.float32).astype(jnp.bfloat16)
            return lax.all_to_all(ordered, "exp", split_axis=0, concat_axis=0, tiled=True)

        def give_back(rows):
            back = lax.all_to_all(rows, "exp", split_axis=0, concat_axis=0, tiled=True)
            return contract_rows(place, back)

        given = (send(tokens), send(grad_out))
        result, grad_local, *rest = run_layer(tok_rows, 0, False, given, *params)
        mixed = (tokens.astype(jnp.float32) + live * give_back(result)).astype(jnp.bfloat16)
        tokens_grad = (cotangent.astype(jnp.float32) + give_back(grad_local)).astype(jnp.bfloat16)
        results = (mixed, tokens_grad, *rest)
    mixed, tokens_grad, gwi, gwo, cent_grad, gain_grad, nbias_grad, bin_grad, bout_grad = results
    return (
        mixed,
        tokens_grad,
        cent_grad,
        gain_grad[None],
        nbias_grad[None],
        gwi[None],
        bin_grad[None],
        gwo[None],
        bout_grad[None],
    )


def solution(mesh):
    placed = (
        P(("rep", "exp"), None),
        P(("rep", "exp"), None),
        P(),
        P("exp", None),
        P("exp", None, None),
        P("exp", None, None),
        P("exp", None, None, "rep"),
        P("exp", None, None),
        P("exp", None, "rep", None),
        P("exp", None, None),
        P(("rep", "exp"), None),
    )
    return jax.shard_map(
        shards,
        mesh=mesh,
        in_specs=placed,
        out_specs=(
            P(("rep", "exp"), None),
            P(("rep", "exp"), None),
            P("exp", None),
            P("exp", None, None),
            P("exp", None, None),
            P("exp", None, None, "rep"),
            P("exp", None, None),
            P("exp", None, "rep", None),
            P("exp", None, None),
        ),
        check_vma=False,
    )
```

profile of v0, /device:TPU:0, one launch (start us, length us, event | category | flops | bytes accessed | tf_op | source)
XLA Modules:
  0.0 404.9 jit_solution(1614509638244636338)
XLA Ops:
  0.7 0.8 select_reduce_fusion
  1.4 0.6 reduce_max.9
  2.7 0.6 conditional.2
  2.7 0.6 branch_0_fun.3
  3.3 401.4 %conditional.3 = (bf16[512,1024]{1,0:T(8,128)(2,1)}, bf16[512,1024]{1,0:T(8,128)(2,1)}, f32[1,1024]{1,0:T(1,128)}, f32[1,2,1024]{2,1,0:T(2,128)}, f32[1,2,1024]{...) conditional(s32[]{:T(128)} %convert_element_type.7, ...), branch_computations={%region_4.5_spmd, %region_5.6_spmd} | conditional | flops 68719476736 | bytes 25174300 | solution.py:1024
  3.3 0.0 copy-start.1
  3.3 0.0 copy-start.3
  3.3 0.0 copy-start.5
  3.3 393.0 %branch_0_fun.4 = (bf16[512,1024]{1,0:T(8,128)(2,1)S(1)}, bf16[512,1024]{1,0:T(8,128)(2,1)S(1)}, f32[2,1024,1024]{2,1,0:T(8,128)S(1)}, f32[2,1024,1024]{2,1,0:T(...) custom-call(bf16[512,1024]{1,0:T(8,128)(2,1)} %get-tuple-element.135, ...), custom_call_target="tpu_custom_call" | custom-call | flops 68719476736 | bytes 20971520 | tf_op jit(solution)/shard_map/cond/branch_0_fun/pallas_call | solution.py:858
  396.3 0.0 copy-done.1
  396.3 0.0 copy-done.3
  396.3 0.0 copy-done.5
  396.3 8.2 %branch_0_fun.5 = (bf16[512,1024]{1,0:T(8,128)(2,1)}, bf16[512,1024]{1,0:T(8,128)(2,1)}, f32[2,1024,1024]{2,1,0:T(8,128)}, f32[2,1024,1024]{2,1,0:T(8,128)}, f32...) custom-call(bf16[512,1024]{1,0:T(8,128)(2,1)S(1)} %copy-done.1, ...), custom_call_target="tpu_custom_call" | custom-call | tf_op jit(solution)/shard_map/cond/branch_0_fun/pallas_call | solution.py:954
  (1 shorter events, 0.0 us)
Async XLA Ops:
  3.3 393.0 %copy-start.1 = (bf16[512,1024]{1,0:T(8,128)(2,1)S(1)}, bf16[512,1024]{1,0:T(8,128)(2,1)}, u32[]{:S(2)}) copy-start(bf16[512,1024]{1,0:T(8,128)(2,1)} %get-tuple-element.135.refs_0_) | copy-start | bytes 3145732 | tf_op jit(solution)/shard_map/cond
  3.3 393.0 %copy-start.3 = (s32[1,512]{1,0:T(1,128)S(1)}, s32[1,512]{1,0:T(1,128)}, u32[]{:S(2)}) copy-start(s32[1,512]{1,0:T(1,128)} %get-tuple-element.137.refs_2_) | copy-start | bytes 6148 | tf_op jit(solution)/shard_map/cond
  3.3 393.0 %copy-start.5 = (s32[8]{0:T(128)S(1)}, s32[8]{0:T(128)}, u32[]{:S(2)}) copy-start(s32[8]{0:T(128)} %get-tuple-element.138.refs_3_) | copy-start | bytes 100 | tf_op jit(solution)/shard_map/cond
where the time goes:
time: 407 us; the launch traced here: 405 us
  Pallas kernels  402 us (99%)
    pallas_call x1, Pallas kernels, run_layer(): pl.pallas_call(functools.partial(kernel, n, blocks, inside, parts), out_s...  393 us
    pallas_call x1, Pallas kernels, close(): pl.pallas_call(functools.partial(close_kernel, n * blocks, rows // blocks...  8.19 us

commit v1 on v0

--- a/solution.py
+++ b/solution.py
@@ -791,7 +791,7 @@
         most = mine[6:7, :128]
         for q in range(1, n):
             most = jnp.maximum(most, peers[q - 1, 6:7, :128])
-        top_out[...] = jnp.broadcast_to(most, top_out.shape)
+        top_out[...] = most[:, 0:1]
     for q in range(1, n):
         tell(1, q).wait_recv()
     mine_rows = mine_late[...]
@@ -868,7 +868,7 @@
             jax.ShapeDtypeStruct((2, n * hidden), full),
             jax.ShapeDtypeStruct((2, width), full),
         )
-        + ((jax.ShapeDtypeStruct((8, 128), full),) if inside else ()),
+        + ((jax.ShapeDtypeStruct((1, 1), full),) if inside else ()),
         in_specs=row_specs + [vmem] * 5 + [anywhere] * 2,
         out_specs=(vmem,) * (10 if inside else 9),
         scratch_shapes=[
@@ -1008,7 +1008,7 @@
 
         def layer(own_rows, name, given, *params):
             *results, most = run_layer(own_rows, name, True, given, *params)
-            return tuple(close(*given, *results)), most[0, 0] <= own_rows
+            return tuple(close(*given, *results)), most.reshape(()) <= own_rows
 
         seqs, planes = lengths.shape[0], lax.axis_size("rep")
         of_plane = lax.iota(jnp.int32, seqs) // (seqs // planes) == lax.iota(jnp.int32, planes)[:, None]

time: 407 us -> 407 us (level)
  no operation moved by 1% of the time
where the time goes in v1:
time: 407 us; the launch traced here: 405 us
  Pallas kernels  402 us (99%)
    pallas_call x1, Pallas kernels, run_layer(): pl.pallas_call(functools.partial(kernel, n, blocks, inside, parts), out_s...  393 us
    pallas_call x1, Pallas kernels, close(): pl.pallas_call(functools.partial(close_kernel, n * blocks, rows // blocks...  8.19 us

profile of v1, /device:TPU:0, one launch (start us, length us, event | category | flops | bytes accessed | tf_op | source)
XLA Modules:
  0.0 405.0 jit_solution(2525605203644336188)
XLA Ops:
  0.7 0.8 select_reduce_fusion
  1.4 0.6 reduce_max.9
  2.7 0.6 conditional.2
  2.7 0.6 branch_0_fun.3
  3.3 401.5 %conditional.3 = (bf16[512,1024]{1,0:T(8,128)(2,1)}, bf16[512,1024]{1,0:T(8,128)(2,1)}, f32[1,1024]{1,0:T(1,128)}, f32[1,2,1024]{2,1,0:T(2,128)}, f32[1,2,1024]{...) conditional(s32[]{:T(128)} %convert_element_type.7, ...), branch_computations={%region_4.5_spmd, %region_5.6_spmd} | conditional | flops 68719476736 | bytes 25174300 | solution.py:1024
  3.3 0.0 copy-start.1
  3.3 0.0 copy-start.3
  3.3 0.0 copy-start.5
  3.3 393.0 %branch_0_fun.4 = (bf16[512,1024]{1,0:T(8,128)(2,1)S(1)}, bf16[512,1024]{1,0:T(8,128)(2,1)S(1)}, f32[2,1024,1024]{2,1,0:T(8,128)S(1)}, f32[2,1024,1024]{2,1,0:T(...) custom-call(bf16[512,1024]{1,0:T(8,128)(2,1)} %get-tuple-element.135, ...), custom_call_target="tpu_custom_call" | custom-call | flops 68719476736 | bytes 20971520 | tf_op jit(solution)/shard_map/cond/branch_0_fun/pallas_call | solution.py:858
  396.3 0.0 copy-done.1
  396.3 0.0 copy-done.3
  396.4 0.0 copy-done.5
  396.4 8.2 %branch_0_fun.5 = (bf16[512,1024]{1,0:T(8,128)(2,1)}, bf16[512,1024]{1,0:T(8,128)(2,1)}, f32[2,1024,1024]{2,1,0:T(8,128)}, f32[2,1024,1024]{2,1,0:T(8,128)}, f32...) custom-call(bf16[512,1024]{1,0:T(8,128)(2,1)S(1)} %copy-done.1, ...), custom_call_target="tpu_custom_call" | custom-call | tf_op jit(solution)/shard_map/cond/branch_0_fun/pallas_call | solution.py:954
  (1 shorter events, 0.0 us)
Async XLA Ops:
  3.3 393.0 %copy-start.1 = (bf16[512,1024]{1,0:T(8,128)(2,1)S(1)}, bf16[512,1024]{1,0:T(8,128)(2,1)}, u32[]{:S(2)}) copy-start(bf16[512,1024]{1,0:T(8,128)(2,1)} %get-tuple-element.135.refs_0_) | copy-start | bytes 3145732 | tf_op jit(solution)/shard_map/cond
  3.3 393.0 %copy-start.3 = (s32[1,512]{1,0:T(1,128)S(1)}, s32[1,512]{1,0:T(1,128)}, u32[]{:S(2)}) copy-start(s32[1,512]{1,0:T(1,128)} %get-tuple-element.137.refs_2_) | copy-start | bytes 6148 | tf_op jit(solution)/shard_map/cond
  3.3 393.0 %copy-start.5 = (s32[8]{0:T(128)S(1)}, s32[8]{0:T(128)}, u32[]{:S(2)}) copy-start(s32[8]{0:T(128)} %get-tuple-element.138.refs_3_) | copy-start | bytes 100 | tf_op jit(solution)/shard_map/cond
